TPU v7x, 256 devices: a whole 4x4x8 slice. The times are simulated.
256 devices in a mesh: region: 16 (over y, x), dp: 16 (over z, core).
Axes of the slice: x: 4, y: 4, z: 8, core: 2. Of those that a mesh axis runs over, the one named last changes fastest.
Arguments:
- positions: float32 [3, 4096, 128], P(None, ('region', 'dp')), may hold values from -1 to 1
- spacing: float32 [4096, 128], P(('region', 'dp')), may hold values from 0.015 to 0.15
- targets: float32 [3, 4096], P(None, ('region', 'dp')), may hold values from 0 to 1
- frequencies: float32 [3, 64], replicated, may hold values from -12 to 12
- seg_region: int32 [16384, 1], P(('region', 'dp')), may hold values from 0 to 15; in each aligned block of 64 rows (0 to 63, 64 to 127, ...) at most 8 rows name the same one
- w_in: bfloat16 [16, 128, 256], P('region'), may hold values from -0.5 to 0.5
- w_hidden: bfloat16 [16, 4, 256, 256], P('region'), may hold values from -0.375 to 0.375
- w_head: bfloat16 [16, 4, 256], P('region'), may hold values from -1 to 1
Outputs:
- pixel_color: float32 [3, 4096], P(None, ('region', 'dp'))
- grad_in: float32 [16, 128, 256], P('region', 'dp')
- grad_hidden: float32 [16, 4, 256, 256], P('region', None, 'dp')
- grad_head: float32 [16, 4, 256], P('region', None, 'dp')
Inputs may be any that keep to these rules, and one draw needn't show every extreme that they name: `seg_region`: among the 64 segments of one device, no region is named more than 8 times, a bound that some block reaches.
All inputs are finite; a program needn't handle non-finite values.
Results may differ from a plain program's by a relative error of at most 0.034.
Values may be sent and summed in bfloat16 or wider, within the bound.
No kernel may reach another device: no remote copies, remote signals or barrier semaphores. Data moves between devices by JAX's collectives and lax.ppermute only.
A program may use at most 128 MiB of HBM per device.

v0:
```python
import math

import jax
import jax.numpy as jnp
from jax import lax
from jax.experimental import pallas as pl
from jax.experimental.pallas import tpu as pltpu
from jax.sharding import PartitionSpec as P

LOSS_GAIN = 64.0
F32 = jnp.float32
BF16 = jnp.bfloat16
NN = (((1,), (0,)), ((), ()))
NT = (((1,), (1,)), ((), ()))
TN = (((0,), (0,)), ((), ()))
VMEM_LIMIT = 40 * 1024 * 1024

REGIONS = 16
SEGS = 64
SEG_LEN = 32
CAP = 8
SLOTS = REGIONS * CAP
RAYS_DEV = 16
ROWS = SLOTS * SEG_LEN
ENC = 128
HID = 256
LAYERS = 4
BLOCK = 80

SIN = (3.141592588, -5.167707194, 2.550035118, -0.5980627511, 0.07724868669)
COS = (0.9999999532, -4.934792829, 4.058411309, -1.331876237, 0.219688854)


def iota(shape, axis):
    return lax.broadcasted_iota(jnp.int32, shape, axis)


def dot(a, b, dims=NN):
    return lax.dot_general(a, b, dims, preferred_element_type=F32)


def split3(x):
    hi = x.astype(BF16)
    rest = x - hi.astype(F32)
    mid = rest.astype(BF16)
    low = (rest - mid.astype(F32)).astype(BF16)
    return hi, mid, low


def pick(x, onehot, dims):
    hi, mid, low = split3(x)
    return dot(hi, onehot, dims) + (dot(mid, onehot, dims) + dot(low, onehot, dims))


def pick_left(onehot, x, dims):
    hi, mid, low = split3(x)
    return dot(onehot, hi, dims) + (dot(onehot, mid, dims) + dot(onehot, low, dims))


def as_mask(cond):
    return jnp.where(cond, 1.0, 0.0).astype(BF16)


def dispatch_kernel(pos_ref, sp_ref, tg_ref, seg_ref, send_ref, meta_ref):
    parity = lax.axis_index("region") % 2
    lane = iota((SEGS, SLOTS), 1)
    row = iota((SEGS, SEGS), 0)
    order = as_mask(iota((SEGS, SEGS), 1) == (row % RAYS_DEV) * 4 + row // RAYS_DEV)
    seg = dot(order, jnp.broadcast_to(seg_ref[...], (8, SEGS)).astype(F32).astype(BF16), NT)[:, 0:1]
    member = jnp.where(seg == lane.astype(F32), 1.0, 0.0)
    earlier = as_mask(iota((SEGS, SEGS), 1) < row)
    rank = dot(earlier, member.astype(BF16))
    slot = jnp.sum(member * (rank + (lane * CAP).astype(F32)), axis=1, keepdims=True)
    onehot = as_mask(slot == lane.astype(F32))
    parts = []
    for q in range(4):
        cut = slice(q * SEG_LEN, (q + 1) * SEG_LEN)
        parts.append(
            jnp.concatenate(
                [pos_ref[0, :, cut], pos_ref[1, :, cut], pos_ref[2, :, cut], sp_ref[:, cut]], axis=1
            )
        )
    data = jnp.concatenate(parts, axis=0)
    send_ref[...] = pick_left(onehot, data, TN)
    ids = dot(iota((8, SLOTS), 1).astype(BF16), onehot, NT)
    half = iota((8, 128), 1) // SEGS == parity
    ids = jnp.concatenate([ids, ids], axis=1)
    spread = as_mask(iota((RAYS_DEV, 128), 1) % RAYS_DEV == iota((RAYS_DEV, 128), 0))
    tg = pick(jnp.concatenate([tg_ref[...], tg_ref[...], tg_ref[0:2, :]], axis=0), spread, NN)
    meta_ref[...] = jnp.where(half, jnp.concatenate([ids[0:4], ids[0:1], tg[0:3]], axis=0), 0.0)


def dispatch(positions, spacing, targets, seg_region):
    return pl.pallas_call(
        dispatch_kernel,
        in_specs=[pl.BlockSpec(memory_space=pltpu.VMEM)] * 4,
        out_shape=(
            jax.ShapeDtypeStruct((SLOTS, 128), F32),
            pltpu.HBM((8, 128), F32),
        ),
        name="dispatch",
    )(positions, spacing, targets, seg_region)


def encode(pos, freq, first, count):
    cols = []
    for t in range(count):
        at = first + t
        cols.append(
            (freq[:, 0:1] * pos(0, at) + freq[:, 1:2] * pos(1, at)) + freq[:, 2:3] * pos(2, at)
        )
    turns = jnp.concatenate(cols, axis=1)
    x = turns - jnp.floor(turns + 0.5)
    y = x * x
    sine = x * (SIN[0] + y * (SIN[1] + y * (SIN[2] + y * (SIN[3] + y * SIN[4]))))
    cosine = COS[0] + y * (COS[1] + y * (COS[2] + y * (COS[3] + y * COS[4])))
    twice = sine + sine
    return jnp.concatenate([twice * cosine, 1.0 - twice * sine], axis=0).astype(BF16)


def local_render(raw, spacing):
    value = raw[0]
    small = jnp.exp(-jnp.abs(value))
    log1p = jnp.where(
        small < 0.02,
        small * (1.0 - small * (0.5 - small * (1.0 / 3.0 - small * 0.25))),
        jnp.log(1.0 + small),
    )
    density = jnp.maximum(value, 0.0) + log1p
    depth = density * spacing
    before = as_mask(iota((SEG_LEN, SEG_LEN), 1) < iota((SEG_LEN, SEG_LEN), 0))
    transmit = jnp.exp(-pick_left(before, depth, NN))
    fade = jnp.exp(-depth)
    opaque = jnp.where(
        depth < 0.03,
        depth * (1.0 - depth * (0.5 - depth * (1.0 / 6.0 - depth * (1.0 / 24.0)))),
        1.0 - fade,
    )
    weight = transmit * opaque
    tints = [0.5 + 0.5 * jnp.tanh(0.5 * raw[c]) for c in (1, 2, 3)]
    return depth, transmit, fade, weight, tints


def forward_kernel(
    recv_ref, meta_ref, freq_ref, win_ref, wh_ref, head_ref,
    send_ref, enc_ref, half_ref, local_ref,
    pos_ref, raw_ref, meta_copy, halves, encoded, local, sem, out_sem, *, chunk,
):
    meta = pltpu.make_async_copy(meta_ref, meta_copy, sem)
    meta.start()
    pos_ref[...] = jnp.transpose(recv_ref[...])
    count = chunk // SLOTS

    def pos(c, at):
        return pos_ref[c * SEG_LEN + at : c * SEG_LEN + at + 1, :]

    starts = range(0, ROWS, chunk)
    acts = []
    for start in starts:
        acts.append(encode(pos, freq_ref[...], start // SLOTS, count))
        encoded[:, start : start + chunk] = acts[-1]
    copies = [pltpu.make_async_copy(encoded, enc_ref, out_sem.at[LAYERS + 1])]
    copies[-1].start()
    for index in range(LAYERS + 1):
        weight = win_ref[...] if index == 0 else wh_ref[index - 1]
        for i, start in enumerate(starts):
            half = dot(weight, acts[i])
            acts[i] = (half + half * jnp.tanh(half)).astype(BF16)
            halves[index, :, start : start + chunk] = half.astype(BF16)
        copies.append(pltpu.make_async_copy(halves.at[index], half_ref.at[index], out_sem.at[index]))
        copies[-1].start()
    for i, act in enumerate(acts):
        raw = dot(head_ref[...], act)
        for t in range(count):
            for c in range(4):
                raw_ref[c, i * count + t : i * count + t + 1, :] = raw[c : c + 1, t * SLOTS : (t + 1) * SLOTS]
    raw = [raw_ref[c] for c in range(4)]
    spacing = pos_ref[3 * SEG_LEN : 4 * SEG_LEN, :]
    depth, transmit, fade, weight, tints = local_render(raw, spacing)
    rows = [jnp.sum(depth, axis=0, keepdims=True)]
    rows += [jnp.sum(weight * tint, axis=0, keepdims=True) for tint in tints]
    meta.wait()
    block = jnp.concatenate(rows + [meta_copy[4:8, :]], axis=0)
    for r in range(REGIONS):
        send_ref[r] = block
    steep = (0.5 + 0.5 * jnp.tanh(0.5 * raw[0])) * spacing
    local[0] = transmit * fade * steep
    local[1] = steep
    for c in range(3):
        local[2 + c] = tints[c]
        local[5 + c] = weight * (tints[c] * (1.0 - tints[c]))
    local[8] = weight
    copies.append(pltpu.make_async_copy(local, local_ref, out_sem.at[LAYERS + 2]))
    copies[-1].start()
    for copy in copies:
        copy.wait()


def in_vmem(count):
    return [pl.BlockSpec(memory_space=pltpu.VMEM)] * count


def in_hbm(count):
    return [pl.BlockSpec(memory_space=pltpu.HBM)] * count


def forward_call(recv, meta, freq, win_t, wh_t, head, chunk=2048):
    kernel = lambda *refs: forward_kernel(*refs, chunk=chunk)
    specs = in_vmem(6)
    specs[1] = in_hbm(1)[0]
    meta = pltpu.with_memory_space_constraint(meta, pltpu.HBM)
    return pl.pallas_call(
        kernel,
        in_specs=specs,
        out_shape=(
            jax.ShapeDtypeStruct((REGIONS, 8, SLOTS), F32),
            pltpu.HBM((ENC, ROWS), BF16),
            pltpu.HBM((LAYERS + 1, HID, ROWS), BF16),
            pltpu.HBM((9, SEG_LEN, SLOTS), F32),
        ),
        out_specs=tuple(in_vmem(1) + in_hbm(3)),
        scratch_shapes=[
            pltpu.VMEM((128, SLOTS), F32),
            pltpu.VMEM((4, SEG_LEN, SLOTS), F32),
            pltpu.VMEM((8, SLOTS), F32),
            pltpu.VMEM((LAYERS + 1, HID, ROWS), BF16),
            pltpu.VMEM((ENC, ROWS), BF16),
            pltpu.VMEM((9, SEG_LEN, SLOTS), F32),
            pltpu.SemaphoreType.DMA,
            pltpu.SemaphoreType.DMA((LAYERS + 3,)),
        ],
        compiler_params=pltpu.CompilerParams(vmem_limit_bytes=VMEM_LIMIT),
        cost_estimate=pl.CostEstimate(flops=2 * ROWS * 296000, bytes_accessed=700000, transcendentals=ROWS * 1280),
        name="forward",
    )(recv, meta, freq, win_t, wh_t, head)


def composite(me, got, gain):
    pairs = REGIONS // 2
    values = jnp.concatenate([got[r] for r in range(REGIONS)], axis=0)
    hi, mid, low = split3(values)
    lane = iota((1, 128), 1)
    sub = iota((128, 128), 0)
    depth_rows, colour_rows, target_rows, onehots = [], [[], [], []], [[], [], []], []
    for m in range(pairs):
        meta = got[2 * m, 4:8, :] + got[2 * m + 1, 4:8, :]
        ids = meta[0:1, :].astype(jnp.int32)
        owner = ids // CAP
        place = (2 * m + lane // SEGS) * CAP + ids % CAP
        onehot = sub == place
        picked = as_mask(onehot)
        found = dot(hi, picked) + (dot(mid, picked) + dot(low, picked))
        total = jnp.zeros((8, 128), F32)
        for r in range(REGIONS):
            total = total + jnp.where(owner == r, found[8 * r : 8 * r + 8], 0.0)
        depth_rows.append(total[0:1])
        for c in range(3):
            colour_rows[c].append(total[1 + c : 2 + c])
            target_rows[c].append(meta[1 + c : 2 + c])
        onehots.append(as_mask(jnp.logical_and(onehot, owner == me)))
    depth = jnp.concatenate(depth_rows, axis=0)
    colours = [jnp.concatenate(rows, axis=0) for rows in colour_rows]
    targets = [jnp.concatenate(rows, axis=0) for rows in target_rows]
    within = iota((pairs, 128), 1) % SEGS

    def earlier(x):
        total = jnp.zeros_like(x)
        for k in (1, 2, 3):
            total = total + jnp.where(within >= k * RAYS_DEV, pltpu.roll(x, k * RAYS_DEV, 1), 0.0)
        return total

    def later(x):
        total = jnp.zeros_like(x)
        for k in (1, 2, 3):
            total = total + jnp.where(within < SEGS - k * RAYS_DEV, pltpu.roll(x, 128 - k * RAYS_DEV, 1), 0.0)
        return total

    transmit = jnp.exp(-earlier(depth))
    behind = jnp.zeros((pairs, 128), F32)
    pixels, scaled = [], []
    for c in range(3):
        weighted = transmit * colours[c]
        after = later(weighted)
        pixel = (earlier(weighted) + weighted) + after
        pull = (pixel - targets[c]) * gain
        behind = behind + pull * after
        scaled.append(transmit * pull)
        pixels.append(pixel)
    rows = scaled + [behind]
    slots = jnp.zeros((32, SLOTS), F32)
    for m in range(pairs):
        x = jnp.concatenate([r[m : m + 1] for r in rows] + [jnp.zeros((4, 128), F32)], axis=0)
        parts = jnp.concatenate([p.astype(F32) for p in split3(x)] + [jnp.zeros((8, 128), F32)], axis=0)
        slots = slots + dot(parts.astype(BF16), onehots[m], NT)
    slots = slots[0:8] + (slots[8:16] + slots[16:24])
    own = []
    mine = jnp.logical_and(iota((pairs, 128), 0) == me // 2, iota((pairs, 128), 1) // SEGS == me % 2)
    for c in range(3):
        row = jnp.sum(jnp.where(mine, pixels[c], 0.0), axis=0, keepdims=True)
        own.append((row + pltpu.roll(row, SEGS, 1))[:, 0:RAYS_DEV])
    return slots, jnp.concatenate(own, axis=0)


def backward_kernel(
    got_ref, wh_ref, head_ref, local_in, enc_in, half_in,
    pix_ref, keep_ref, send_ref, up_ref, gin_ref, gh_ref, halves, enc_ref, local_ref, in_sem, *, chunk, gain,
):
    copies = [
        pltpu.make_async_copy(half_in.at[index], halves.at[index], in_sem.at[index])
        for index in range(LAYERS + 1)
    ]
    local_copy = pltpu.make_async_copy(local_in, local_ref, in_sem.at[LAYERS + 1])
    enc_copy = pltpu.make_async_copy(enc_in, enc_ref, in_sem.at[LAYERS + 2])
    for copy in [local_copy] + copies[::-1] + [enc_copy]:
        copy.start()
    slots, pixel = composite(lax.axis_index("region"), got_ref, gain)
    pix_ref[...] = pixel
    local_copy.wait()
    pull = jnp.zeros((SEG_LEN, SLOTS), F32)
    for c in range(3):
        pull = pull + slots[c : c + 1] * local_ref[2 + c]
    after = as_mask(iota((SEG_LEN, SEG_LEN), 1) > iota((SEG_LEN, SEG_LEN), 0))
    rest = pick_left(after, local_ref[8] * pull, NN) + slots[3:4]
    ups = [local_ref[0] * pull - rest * local_ref[1]]
    ups += [slots[c : c + 1] * local_ref[5 + c] for c in range(3)]
    up_ref[...] = jnp.zeros_like(up_ref)
    for c in range(4):
        for t in range(SEG_LEN):
            up_ref[c : c + 1, t * SLOTS : (t + 1) * SLOTS] = ups[c][t : t + 1]

    cuts = [slice(start, start + chunk) for start in range(0, ROWS, chunk)]

    def residual(index, cut):
        half = halves[index, :, cut]
        tanh = jnp.tanh(half)
        above = 1.0 + tanh
        return half * above, above + half * (above * (1.0 - tanh))

    copies[LAYERS].wait()
    flows, slopes = [], []
    ghead = jnp.zeros((8, HID), F32)
    for cut in cuts:
        up = up_ref[:, cut].astype(BF16)
        flows.append(dot(head_ref[...], up))
        act, slope = residual(LAYERS, cut)
        slopes.append(slope)
        ghead = ghead + dot(up, act, NT)
    for index in range(LAYERS, -1, -1):
        if index > 0:
            copies[index - 1].wait()
        else:
            enc_copy.wait()
        total = None
        for i, cut in enumerate(cuts):
            back = flows[i].astype(BF16) * slopes[i]
            if index > 0:
                flows[i] = dot(wh_ref[index - 1], back)
                act, slopes[i] = residual(index - 1, cut)
            else:
                act = enc_ref[:, cut]
            part = dot(act, back, NT)
            total = part if total is None else total + part
        if index > 0:
            gh_ref[index - 1] = total
        else:
            gin_ref[...] = total
    core = lax.axis_index("dp") % 2
    for ref, which in ((keep_ref, core), (send_ref, 1 - core)):
        for z in range(8):
            to = z * 2 + which
            for l in range(LAYERS):
                rows = gh_ref[l, pl.ds(pl.multiple_of(to * 16, 16), 16), :]
                ref[z, l * 16 : (l + 1) * 16, :] = rows.astype(BF16)
            rows = gin_ref[pl.ds(pl.multiple_of(to * 8, 8), 8), :]
            ref[z, 64:80, :] = jnp.concatenate([rows, ghead], axis=0).astype(BF16)


def backward_call(got, wh, head, local, enc, half, gain, chunk=2048):
    held = [pltpu.with_memory_space_constraint(x, pltpu.HBM) for x in (local, enc, half)]
    kernel = lambda *refs: backward_kernel(*refs, chunk=chunk, gain=gain)
    return pl.pallas_call(
        kernel,
        in_specs=in_vmem(3) + in_hbm(3),
        out_shape=(
            jax.ShapeDtypeStruct((3, RAYS_DEV), F32),
            jax.ShapeDtypeStruct((8, BLOCK, HID), BF16),
            jax.ShapeDtypeStruct((8, BLOCK, HID), BF16),
        ),
        scratch_shapes=[
            pltpu.VMEM((8, ROWS), F32),
            pltpu.VMEM((ENC, HID), F32),
            pltpu.VMEM((LAYERS, HID, HID), F32),
            pltpu.VMEM((LAYERS + 1, HID, ROWS), BF16),
            pltpu.VMEM((ENC, ROWS), BF16),
            pltpu.VMEM((9, SEG_LEN, SLOTS), F32),
            pltpu.SemaphoreType.DMA((LAYERS + 3,)),
        ],
        compiler_params=pltpu.CompilerParams(vmem_limit_bytes=VMEM_LIMIT),
        cost_estimate=pl.CostEstimate(flops=4 * ROWS * 296000, bytes_accessed=23000000, transcendentals=0),
        name="backward",
    )(got, wh, head, *held)


def total_kernel(got_ref, gin_ref, gh_ref, ghead_ref):
    total = got_ref[0].astype(F32)
    for z in range(1, 8):
        total = total + got_ref[z].astype(F32)
    for l in range(LAYERS):
        gh_ref[0, l] = total[l * 16 : (l + 1) * 16]
    gin_ref[0] = total[64:72]
    mine = iota((HID, 16), 0) == lax.axis_index("dp") * 16 + iota((HID, 16), 1)
    ghead_ref[0] = pick(total[72:80], as_mask(mine), NN)[0:4]


def total_call(got):
    return pl.pallas_call(
        total_kernel,
        in_specs=in_vmem(1),
        out_shape=(
            jax.ShapeDtypeStruct((1, 8, HID), F32),
            jax.ShapeDtypeStruct((1, LAYERS, 16, HID), F32),
            jax.ShapeDtypeStruct((1, 4, 16), F32),
        ),
        name="total",
    )(got)


def per_device(positions, spacing, targets, frequencies, seg_region, w_in, w_hidden, w_head):
    rays = spacing.shape[0] * lax.axis_size("region") * lax.axis_size("dp")
    gain = LOSS_GAIN / math.sqrt(rays)

    half = jnp.asarray(0.5, BF16)
    win_t = w_in[0].T * half
    wh_t = jnp.transpose(w_hidden[0], (0, 2, 1)) * half
    wh_half = w_hidden[0] * half
    head = w_head[0]
    head_t = jnp.pad(head, ((0, 4), (0, 0))).T * half
    freq = frequencies.T

    outgoing, meta = dispatch(positions, spacing, targets, seg_region.reshape(1, SEGS))
    arrived = lax.all_to_all(
        outgoing.reshape(REGIONS, CAP, 128), "region", split_axis=0, concat_axis=0, tiled=True
    ).reshape(SLOTS, 128)
    summary, enc, half_pre, local = forward_call(arrived, meta, freq, win_t, wh_t, head)
    got = lax.all_to_all(summary, "region", split_axis=0, concat_axis=0, tiled=True)
    pixel_color, keep, send = backward_call(got, wh_half, head_t, local, enc, half_pre, gain)
    other = lax.ppermute(send, "dp", [(i, i ^ 1) for i in range(16)])
    both = (keep.astype(F32) + other.astype(F32)).astype(BF16)
    groups = [list(range(0, 16, 2)), list(range(1, 16, 2))]
    parts = lax.all_to_all(both, "dp", 0, 0, tiled=True, axis_index_groups=groups)
    grad_in, grad_hidden, grad_head = total_call(parts)
    return pixel_color, grad_in, grad_hidden, grad_head


def solution(mesh):
    return jax.shard_map(
        per_device,
        mesh=mesh,
        in_specs=(
            P(None, ("region", "dp"), None),
            P(("region", "dp"), None),
            P(None, ("region", "dp")),
            P(),
            P(("region", "dp"), None),
            P("region", None, None),
            P("region", None, None, None),
            P("region", None, None),
        ),
        out_specs=(
            P(None, ("region", "dp")),
            P("region", "dp", None),
            P("region", None, "dp", None),
            P("region", None, "dp"),
        ),
        check_vma=False,
    )
```

profile of v0, /device:TPU:1, one launch (start us, length us, event | category | flops | bytes accessed | tf_op | source)
XLA Modules:
  0.0 72.7 jit_solution(14515543376795072308)
XLA Ops:
  0.6 2.0 %dispatch.1 = (f32[128,128]{1,0:T(8,128)}, f32[8,128]{1,0:T(8,128)}) custom-call(f32[3,16,128]{2,1,0:T(8,128)} %pos_ref.1, f32[16,128]{1,0:T(8,128)} %sp_ref.1, f32[3,16]{1,0:T(4,128)} %tg_ref.1, s32[1,64]{1,0:T(1,128)} %bitcast.21), custom_call_target="tpu_custom_call" | custom-call | tf_op jit(solution)/shard_map/dispatch/pallas_call | solution.py:94
  2.6 7.6 %all-to-all-start = ((f32[16,8,128]{2,1,0:T(8,128)}), f32[16,8,128]{2,1,0:T(8,128)S(1)}, u32[]{:S(2)}, u32[]{:S(2)}) async-start(f32[16,8,128]{2,1,0:T(8,128)} %bitcast.20), calls=%async_computation | async-start | bytes 131072 | tf_op jit(solution)/shard_map/all_to_all | solution.py:441
  10.2 1.0 %copy.13 = bf16[1,128,256]{1,2,0:T(8,128)(2,1)S(1)} copy(bf16[1,128,256]{2,1,0:T(8,128)(2,1)} %param.13) | data formatting | bytes 131072 | tf_op args[5]
  11.2 1.1 %multiply_bitcast_fusion.1 = (bf16[4,256,256]{2,1,0:T(8,128)(2,1)S(1)}, bf16[4,256,256]{1,2,0:T(8,128)(2,1)S(1)}) fusion(bf16[1,4,256,256]{3,2,1,0:T(8,128)(2,1)} %param.14), kind=kLoop, calls=%fused_computation.2 | loop fusion | flops 262144 | bytes 1572864 | tf_op jit(solution)/shard_map/mul | solution.py:434
  12.3 0.8 %copy.12 = f32[3,64]{0,1:T(8,128)S(1)} copy(f32[3,64]{1,0:T(4,128)} %param.11) | data formatting | bytes 1536 | tf_op args[3]
  13.1 0.8 %copy.14 = bf16[1,4,256]{1,2,0:T(8,128)(2,1)S(1)} copy(bf16[1,4,256]{2,1,0:T(4,128)(2,1)} %param.15) | data formatting | bytes 4096 | tf_op args[7]
  13.9 0.1 copy.16.refs_5_
  14.0 0.2 copy.15.refs_4_
  14.2 2.5 %all-to-all-done = f32[16,8,128]{2,1,0:T(8,128)S(1)} async-done(((f32[16,8,128]{2,1,0:T(8,128)}), f32[16,8,128]{2,1,0:T(8,128)S(1)}, u32[]{:S(2)}, u32[]{:S(2)}) %all-to-all-start) | async-done | bytes 65568 | tf_op jit(solution)/shard_map/all_to_all | solution.py:441
  16.8 7.6 %forward.1 = (f32[16,8,128]{2,1,0:T(8,128)}, bf16[128,4096]{1,0:T(8,128)(2,1)}, bf16[5,256,4096]{2,1,0:T(8,128)(2,1)}, f32[9,32,128]{2,1,0:T(8,128)}) custom-call(f32[128,128]{1,0:T(8,128)S(1)} %bitcast.16, f32[8,128]{1,0:T(8,128)} %get-tuple-element.17.refs_1_, f32[64,3]{1,0:T(8,128)S(1)} %bitcast.17, bf16[256,128]{1,0:T(8,128)(2,1)S(1)} %multiply_bitcast_fusion.3.refs_3_, ...), custom_call_target="tpu_custom_call" | custom-call | flops 2424832000 | bytes 700000 | tf_op jit(solution)/shard_map/forward/pallas_call | solution.py:212
  24.3 4.2 %all-to-all-start.1 = ((f32[16,8,128]{2,1,0:T(8,128)}), f32[16,8,128]{2,1,0:T(8,128)S(1)}, u32[]{:S(2)}, u32[]{:S(2)}) async-start(f32[16,8,128]{2,1,0:T(8,128)} %get-tuple-element.18), calls=%async_computation.1 | async-start | bytes 131072 | tf_op jit(solution)/shard_map/all_to_all | solution.py:445
  28.5 6.5 %all-to-all-done.1.refs_0_ = f32[16,8,128]{2,1,0:T(8,128)S(1)} async-done(((f32[16,8,128]{2,1,0:T(8,128)}), f32[16,8,128]{2,1,0:T(8,128)S(1)}, u32[]{:S(2)}, u32[]{:S(2)}) %all-to-all-start.1) | async-done | bytes 65568 | tf_op jit(solution)/shard_map/all_to_all | solution.py:445
  35.0 11.0 %backward.1 = (f32[3,16]{1,0:T(4,128)}, bf16[8,80,256]{2,1,0:T(8,128)(2,1)S(1)}, bf16[8,80,256]{2,1,0:T(8,128)(2,1)S(1)}) custom-call(f32[16,8,128]{2,1,0:T(8,128)S(1)} %all-to-all-done.1.refs_0_, bf16[4,256,256]{2,1,0:T(8,128)(2,1)S(1)} %get-tuple-element.28.refs_1_, bf16[256,8]{1,0:T(8,128)(2,1)S(1)} %multiply_bitcast_fusion.2.refs_2_, ...), custom_call_target="tpu_custom_call" | custom-call | flops 4849664000 | bytes 23000000 | tf_op jit(solution)/shard_map/backward/pallas_call | solution.py:381
  46.0 2.8 %collective-permute-start = (bf16[8,80,256]{2,1,0:T(8,128)(2,1)S(1)}, bf16[8,80,256]{2,1,0:T(8,128)(2,1)S(1)}, u32[]{:S(2)}, u32[]{:S(2)}) collective-permute-start(bf16[8,80,256]{2,1,0:T(8,128)(2,1)S(1)} %get-tuple-element.24), channel_id=1, source_target_pairs={{0,1},{1,0},{2,3},{3,2},{4,5},{5,4},{6,7},{7,6},{8,9},{9,8},{10,11... | collective-permute-start | bytes 983048 | tf_op jit(solution)/shard_map/ppermute | solution.py:447
  48.8 1.3 %collective-permute-done = bf16[8,80,256]{2,1,0:T(8,128)(2,1)S(1)} collective-permute-done((bf16[8,80,256]{2,1,0:T(8,128)(2,1)S(1)}, bf16[8,80,256]{2,1,0:T(8,128)(2,1)S(1)}, u32[]{:S(2)}, u32[]{:S(2)}) %collective-permute-start) | collective-permute-done | bytes 327712 | tf_op jit(solution)/shard_map/ppermute | solution.py:447
  50.1 0.1 add_convert_fusion
  50.1 20.9 %all_to_all.15.got_ref = bf16[8,80,256]{2,1,0:T(8,128)(2,1)} all-to-all(bf16[8,80,256]{2,1,0:T(8,128)(2,1)S(1)} %add_convert_fusion), channel_id=1, replica_groups={{0,2,4,6,8,10,12,14},{1,3,5,7,9,11,13,15},{16,18,20,22,24,26,28,30},{17..., dimensions={0} | all-to-all | bytes 655360 | tf_op jit(solution)/shard_map/all_to_all | solution.py:450
  71.0 1.7 %total.1 = (f32[1,8,256]{2,1,0:T(8,128)}, f32[1,4,16,256]{3,2,1,0:T(8,128)}, f32[1,4,16]{2,1,0:T(4,128)}) custom-call(bf16[8,80,256]{2,1,0:T(8,128)(2,1)} %all_to_all.15.got_ref), custom_call_target="tpu_custom_call" | custom-call | tf_op jit(solution)/shard_map/total/pallas_call | solution.py:416
  (2 shorter events, 0.0 us)
Async XLA Ops:
  2.6 14.1 %all-to-all-start = ((f32[16,8,128]{2,1,0:T(8,128)}), f32[16,8,128]{2,1,0:T(8,128)S(1)}, u32[]{:S(2)}, u32[]{:S(2)}) async-start(f32[16,8,128]{2,1,0:T(8,128)} %bitcast.20), calls=%async_computation | async-start | bytes 131072 | tf_op jit(solution)/shard_map/all_to_all | solution.py:441
  24.3 10.7 %all-to-all-start.1 = ((f32[16,8,128]{2,1,0:T(8,128)}), f32[16,8,128]{2,1,0:T(8,128)S(1)}, u32[]{:S(2)}, u32[]{:S(2)}) async-start(f32[16,8,128]{2,1,0:T(8,128)} %get-tuple-element.18), calls=%async_computation.1 | async-start | bytes 131072 | tf_op jit(solution)/shard_map/all_to_all | solution.py:445
  46.0 4.0 %collective-permute-start = (bf16[8,80,256]{2,1,0:T(8,128)(2,1)S(1)}, bf16[8,80,256]{2,1,0:T(8,128)(2,1)S(1)}, u32[]{:S(2)}, u32[]{:S(2)}) collective-permute-start(bf16[8,80,256]{2,1,0:T(8,128)(2,1)S(1)} %get-tuple-element.24), channel_id=1, source_target_pairs={{0,1},{1,0},{2,3},{3,2},{4,5},{5,4},{6,7},{7,6},{8,9},{9,8},{10,11... | collective-permute-start | bytes 983048 | tf_op jit(solution)/shard_map/ppermute | solution.py:447
where the time goes:
time: 73.2 us; the launch traced here: 72.7 us
  Pallas kernels  22.3 us (30%)
  blocking collectives  20.9 us (29%)
  starting transfers between devices  14.5 us (20%)
  waiting for transfers between devices  10.3 us (14%)
  local copies, waits for them, and re-layouts  2.85 us (4%)
  other arithmetic  1.23 us (2%)
    all_to_all x1, blocking collectives, per_device(): lax.all_to_all(both, 'dp', 0, 0, tiled=True, axis_index_groups=groups)  20.9 us
    pallas_call x1, Pallas kernels, backward_call(): pl.pallas_call(kernel, in_specs=in_vmem(3) + in_hbm(3), out_shape=(jax.Sh...  11 us
    all_to_all x1, starting transfers between devices, per_device(): lax.all_to_all(outgoing.reshape(REGIONS, CAP, 128), 'region', split_axis=...  7.58 us
    pallas_call x1, Pallas kernels, forward_call(): pl.pallas_call(kernel, in_specs=specs, out_shape=(jax.ShapeDtypeStruct((R...  7.56 us
    all_to_all x1, waiting for transfers between devices, per_device(): lax.all_to_all(summary, 'region', split_axis=0, concat_axis=0, tiled=True)  6.48 us
    all_to_all x1, starting transfers between devices, per_device(): lax.all_to_all(summary, 'region', split_axis=0, concat_axis=0, tiled=True)  4.17 us
    ppermute x1, starting transfers between devices, per_device(): other = lax.ppermute(send, 'dp', [(i, i ^ 1) for i in range(16)])  2.75 us
    unnamed x3, local copies, waits for them, and re-layouts  2.54 us
  transfers between devices with their start and end apart: 3, of which 3 were waited for; matrix products, arithmetic and copies ran while one was open for 5% of the time, Pallas kernels for 0%

commit v1 on v0

--- a/solution.py
+++ b/solution.py
@@ -14,6 +14,7 @@
 NT = (((1,), (1,)), ((), ()))
 TN = (((0,), (0,)), ((), ()))
 VMEM_LIMIT = 40 * 1024 * 1024
+BACK_LIMIT = 24 * 1024 * 1024
 
 REGIONS = 16
 SEGS = 64
@@ -301,21 +302,51 @@
     return slots, jnp.concatenate(own, axis=0)
 
 
+def residual_of(half):
+    tanh = jnp.tanh(half)
+    above = 1.0 + tanh
+    return half * above, above + half * (above * (1.0 - tanh))
+
+
+def fetch_kernel(local_in, half_in, local_ref, top_ref, sem):
+    copies = [
+        pltpu.make_async_copy(half_in.at[LAYERS], top_ref, sem.at[0]),
+        pltpu.make_async_copy(local_in, local_ref, sem.at[1]),
+    ]
+    for copy in copies:
+        copy.start()
+    for copy in copies:
+        copy.wait()
+
+
+def fetch_call(local, half):
+    return pl.pallas_call(
+        fetch_kernel,
+        in_specs=in_hbm(2),
+        out_specs=tuple(in_vmem(2)),
+        out_shape=(
+            jax.ShapeDtypeStruct((9, SEG_LEN, SLOTS), F32),
+            jax.ShapeDtypeStruct((HID, ROWS), BF16),
+        ),
+        scratch_shapes=[pltpu.SemaphoreType.DMA((2,))],
+        compiler_params=pltpu.CompilerParams(vmem_limit_bytes=16 * 1024 * 1024),
+        cost_estimate=pl.CostEstimate(flops=2 * 10**9, bytes_accessed=2 * 10**7, transcendentals=0),
+        name="fetch",
+    )(*[pltpu.with_memory_space_constraint(x, pltpu.HBM) for x in (local, half)])
+
+
 def backward_kernel(
-    got_ref, wh_ref, head_ref, local_in, enc_in, half_in,
-    pix_ref, keep_ref, send_ref, up_ref, gin_ref, gh_ref, halves, enc_ref, local_ref, in_sem, *, chunk, gain,
+    got_ref, wh_ref, head_ref, local_ref, top_ref, enc_in, half_in,
+    pix_ref, keep_ref, send_ref, up_ref, gin_ref, gh_ref, halves, enc_ref, in_sem, *, chunk, gain,
 ):
     copies = [
-        pltpu.make_async_copy(half_in.at[index], halves.at[index], in_sem.at[index])
-        for index in range(LAYERS + 1)
+        pltpu.make_async_copy(half_in.at[index], halves.at[index], in_sem.at[index]) for index in range(LAYERS)
     ]
-    local_copy = pltpu.make_async_copy(local_in, local_ref, in_sem.at[LAYERS + 1])
-    enc_copy = pltpu.make_async_copy(enc_in, enc_ref, in_sem.at[LAYERS + 2])
-    for copy in [local_copy] + copies[::-1] + [enc_copy]:
+    copies.append(pltpu.make_async_copy(enc_in, enc_ref, in_sem.at[LAYERS]))
+    for copy in copies[LAYERS - 1 :: -1] + copies[LAYERS:]:
         copy.start()
     slots, pixel = composite(lax.axis_index("region"), got_ref, gain)
     pix_ref[...] = pixel
-    local_copy.wait()
     pull = jnp.zeros((SEG_LEN, SLOTS), F32)
     for c in range(3):
         pull = pull + slots[c : c + 1] * local_ref[2 + c]
@@ -331,12 +362,9 @@
     cuts = [slice(start, start + chunk) for start in range(0, ROWS, chunk)]
 
     def residual(index, cut):
-        half = halves[index, :, cut]
-        tanh = jnp.tanh(half)
-        above = 1.0 + tanh
-        return half * above, above + half * (above * (1.0 - tanh))
-
-    copies[LAYERS].wait()
+        half = top_ref[:, cut] if index == LAYERS else halves[index, :, cut]
+        return residual_of(half)
+
     flows, slopes = [], []
     ghead = jnp.zeros((8, HID), F32)
     for cut in cuts:
@@ -346,10 +374,8 @@
         slopes.append(slope)
         ghead = ghead + dot(up, act, NT)
     for index in range(LAYERS, -1, -1):
-        if index > 0:
-            copies[index - 1].wait()
-        else:
-            enc_copy.wait()
+        for copy in {LAYERS: copies[LAYERS - 1 : LAYERS], LAYERS - 1: copies[1 : LAYERS - 1], 1: [copies[0], copies[LAYERS]]}.get(index, []):
+            copy.wait()
         total = None
         for i, cut in enumerate(cuts):
             back = flows[i].astype(BF16) * slopes[i]
@@ -375,12 +401,12 @@
             ref[z, 64:80, :] = jnp.concatenate([rows, ghead], axis=0).astype(BF16)
 
 
-def backward_call(got, wh, head, local, enc, half, gain, chunk=2048):
-    held = [pltpu.with_memory_space_constraint(x, pltpu.HBM) for x in (local, enc, half)]
+def backward_call(got, wh, head, local, top, enc, half, gain, chunk=512):
+    enc, half = [pltpu.with_memory_space_constraint(x, pltpu.HBM) for x in (enc, half)]
     kernel = lambda *refs: backward_kernel(*refs, chunk=chunk, gain=gain)
     return pl.pallas_call(
         kernel,
-        in_specs=in_vmem(3) + in_hbm(3),
+        in_specs=in_vmem(5) + in_hbm(2),
         out_shape=(
             jax.ShapeDtypeStruct((3, RAYS_DEV), F32),
             jax.ShapeDtypeStruct((8, BLOCK, HID), BF16),
@@ -390,15 +416,14 @@
             pltpu.VMEM((8, ROWS), F32),
             pltpu.VMEM((ENC, HID), F32),
             pltpu.VMEM((LAYERS, HID, HID), F32),
-            pltpu.VMEM((LAYERS + 1, HID, ROWS), BF16),
+            pltpu.VMEM((LAYERS, HID, ROWS), BF16),
             pltpu.VMEM((ENC, ROWS), BF16),
-            pltpu.VMEM((9, SEG_LEN, SLOTS), F32),
-            pltpu.SemaphoreType.DMA((LAYERS + 3,)),
+            pltpu.SemaphoreType.DMA((LAYERS + 1,)),
         ],
-        compiler_params=pltpu.CompilerParams(vmem_limit_bytes=VMEM_LIMIT),
+        compiler_params=pltpu.CompilerParams(vmem_limit_bytes=BACK_LIMIT),
         cost_estimate=pl.CostEstimate(flops=4 * ROWS * 296000, bytes_accessed=23000000, transcendentals=0),
         name="backward",
-    )(got, wh, head, *held)
+    )(got, wh, head, local, top, enc, half)
 
 
 def total_kernel(got_ref, gin_ref, gh_ref, ghead_ref):
@@ -443,7 +468,8 @@
     ).reshape(SLOTS, 128)
     summary, enc, half_pre, local = forward_call(arrived, meta, freq, win_t, wh_t, head)
     got = lax.all_to_all(summary, "region", split_axis=0, concat_axis=0, tiled=True)
-    pixel_color, keep, send = backward_call(got, wh_half, head_t, local, enc, half_pre, gain)
+    local, top = fetch_call(local, half_pre)
+    pixel_color, keep, send = backward_call(got, wh_half, head_t, local, top, enc, half_pre, gain)
     other = lax.ppermute(send, "dp", [(i, i ^ 1) for i in range(16)])
     both = (keep.astype(F32) + other.astype(F32)).astype(BF16)
     groups = [list(range(0, 16, 2)), list(range(1, 16, 2))]

time: 73.2 us -> 71.2 us (0.973)
  waiting for transfers between devices: 10.3 us -> 8.63 us
    all_to_all x1, waiting for transfers between devices: 6.48 us -> 4.89 us  [per_device(): lax.all_to_all(summary, 'region', split_axis=0, concat_axis=0, tiled=True)]
    pallas_call x1 -> x2, Pallas kernels: 11 us -> 10.5 us  [the longest x1 8.92 us: backward_call(): pl.pallas_call(kernel, in_specs=in_vmem(5) + in_hbm(2), out_shape=(jax.Sh...]
  transfers between devices with their start and end apart: 3 -> 3, of which waited for: 3 -> 3; matrix products, arithmetic and copies ran while one was open for 5% -> 6% of each run, Pallas kernels for 0% -> 2%
where the time goes in v1:
time: 71.2 us; the launch traced here: 70.7 us
  Pallas kernels  21.8 us (31%)
  blocking collectives  20.9 us (29%)
  starting transfers between devices  14.5 us (20%)
  waiting for transfers between devices  8.63 us (12%)
  local copies, waits for them, and re-layouts  2.83 us (4%)
  other arithmetic  1.25 us (2%)
    all_to_all x1, blocking collectives, per_device(): lax.all_to_all(both, 'dp', 0, 0, tiled=True, axis_index_groups=groups)  20.9 us
    pallas_call x1, Pallas kernels, backward_call(): pl.pallas_call(kernel, in_specs=in_vmem(5) + in_hbm(2), out_shape=(jax.Sh...  8.92 us
    all_to_all x1, starting transfers between devices, per_device(): lax.all_to_all(outgoing.reshape(REGIONS, CAP, 128), 'region', split_axis=...  7.58 us
    pallas_call x1, Pallas kernels, forward_call(): pl.pallas_call(kernel, in_specs=specs, out_shape=(jax.ShapeDtypeStruct((R...  7.57 us
    all_to_all x1, waiting for transfers between devices, per_device(): lax.all_to_all(summary, 'region', split_axis=0, concat_axis=0, tiled=True)  4.89 us
    all_to_all x1, starting transfers between devices, per_device(): lax.all_to_all(summary, 'region', split_axis=0, concat_axis=0, tiled=True)  4.2 us
    ppermute x1, starting transfers between devices, per_device(): other = lax.ppermute(send, 'dp', [(i, i ^ 1) for i in range(16)])  2.76 us
    unnamed x3, local copies, waits for them, and re-layouts  2.54 us
  transfers between devices with their start and end apart: 3, of which 3 were waited for; matrix products, arithmetic and copies ran while one was open for 6% of the time, Pallas kernels for 2%

profile of v1, /device:TPU:1, one launch (start us, length us, event | category | flops | bytes accessed | tf_op | source)
XLA Modules:
  0.0 70.7 jit_solution(11754866028861727466)
XLA Ops:
  0.6 2.0 %dispatch.1 = (f32[128,128]{1,0:T(8,128)}, f32[8,128]{1,0:T(8,128)}) custom-call(f32[3,16,128]{2,1,0:T(8,128)} %pos_ref.1, f32[16,128]{1,0:T(8,128)} %sp_ref.1, f32[3,16]{1,0:T(4,128)} %tg_ref.1, s32[1,64]{1,0:T(1,128)} %bitcast.21), custom_call_target="tpu_custom_call" | custom-call | tf_op jit(solution)/shard_map/dispatch/pallas_call | solution.py:95
  2.6 7.6 %all-to-all-start = ((f32[16,8,128]{2,1,0:T(8,128)}), f32[16,8,128]{2,1,0:T(8,128)S(1)}, u32[]{:S(2)}, u32[]{:S(2)}) async-start(f32[16,8,128]{2,1,0:T(8,128)} %bitcast.20), calls=%async_computation | async-start | bytes 131072 | tf_op jit(solution)/shard_map/all_to_all | solution.py:466
  10.2 0.8 %copy.12 = f32[3,64]{0,1:T(8,128)S(1)} copy(f32[3,64]{1,0:T(4,128)} %param.11) | data formatting | bytes 1536 | tf_op args[3]
  11.0 0.9 %copy.13 = bf16[1,128,256]{1,2,0:T(8,128)(2,1)S(1)} copy(bf16[1,128,256]{2,1,0:T(8,128)(2,1)} %param.13) | data formatting | bytes 131072 | tf_op args[5]
  12.0 0.8 %copy.14 = bf16[1,4,256]{1,2,0:T(8,128)(2,1)S(1)} copy(bf16[1,4,256]{2,1,0:T(4,128)(2,1)} %param.15) | data formatting | bytes 4096 | tf_op args[7]
  12.8 0.1 copy.16.refs_5_
  12.9 1.1 %multiply_bitcast_fusion.1 = (bf16[4,256,256]{2,1,0:T(8,128)(2,1)S(1)}, bf16[4,256,256]{1,2,0:T(8,128)(2,1)S(1)}) fusion(bf16[1,4,256,256]{3,2,1,0:T(8,128)(2,1)} %param.14), kind=kLoop, calls=%fused_computation.2 | loop fusion | flops 262144 | bytes 1572864 | tf_op jit(solution)/shard_map/mul | solution.py:459
  14.0 0.2 copy.15.refs_4_
  14.3 2.5 %all-to-all-done = f32[16,8,128]{2,1,0:T(8,128)S(1)} async-done(((f32[16,8,128]{2,1,0:T(8,128)}), f32[16,8,128]{2,1,0:T(8,128)S(1)}, u32[]{:S(2)}, u32[]{:S(2)}) %all-to-all-start) | async-done | bytes 65568 | tf_op jit(solution)/shard_map/all_to_all | solution.py:466
  16.8 7.6 %forward.1 = (f32[16,8,128]{2,1,0:T(8,128)}, bf16[128,4096]{1,0:T(8,128)(2,1)}, bf16[5,256,4096]{2,1,0:T(8,128)(2,1)}, f32[9,32,128]{2,1,0:T(8,128)}) custom-call(f32[128,128]{1,0:T(8,128)S(1)} %bitcast.16, f32[8,128]{1,0:T(8,128)} %get-tuple-element.19.refs_1_, f32[64,3]{1,0:T(8,128)S(1)} %bitcast.17, bf16[256,128]{1,0:T(8,128)(2,1)S(1)} %multiply_bitcast_fusion.3.refs_3_, ...), custom_call_target="tpu_custom_call" | custom-call | flops 2424832000 | bytes 700000 | tf_op jit(solution)/shard_map/forward/pallas_call | solution.py:213
  24.3 4.2 %all-to-all-start.1 = ((f32[16,8,128]{2,1,0:T(8,128)}), f32[16,8,128]{2,1,0:T(8,128)S(1)}, u32[]{:S(2)}, u32[]{:S(2)}) async-start(f32[16,8,128]{2,1,0:T(8,128)} %get-tuple-element.20), calls=%async_computation.1 | async-start | bytes 131072 | tf_op jit(solution)/shard_map/all_to_all | solution.py:470
  28.5 1.6 %fetch.1 = (f32[9,32,128]{2,1,0:T(8,128)S(1)}, bf16[256,4096]{1,0:T(8,128)(2,1)S(1)}) custom-call(f32[9,32,128]{2,1,0:T(8,128)} %get-tuple-element.21.local_in, bf16[5,256,4096]{2,1,0:T(8,128)(2,1)} %get-tuple-element.22.half_in.refs_6_), custom_call_target="tpu_custom_call" | custom-call | flops 2000000000 | bytes 20000000 | tf_op jit(solution)/shard_map/fetch/pallas_call | solution.py:323
  30.2 4.9 %all-to-all-done.1.refs_0_ = f32[16,8,128]{2,1,0:T(8,128)S(1)} async-done(((f32[16,8,128]{2,1,0:T(8,128)}), f32[16,8,128]{2,1,0:T(8,128)S(1)}, u32[]{:S(2)}, u32[]{:S(2)}) %all-to-all-start.1) | async-done | bytes 65568 | tf_op jit(solution)/shard_map/all_to_all | solution.py:470
  35.1 8.9 %backward.1 = (f32[3,16]{1,0:T(4,128)}, bf16[8,80,256]{2,1,0:T(8,128)(2,1)S(1)}, bf16[8,80,256]{2,1,0:T(8,128)(2,1)S(1)}) custom-call(f32[16,8,128]{2,1,0:T(8,128)S(1)} %all-to-all-done.1.refs_0_, bf16[4,256,256]{2,1,0:T(8,128)(2,1)S(1)} %get-tuple-element.32.refs_1_, bf16[256,8]{1,0:T(8,128)(2,1)S(1)} %multiply_bitcast_fusion.2.refs_2_, ...), custom_call_target="tpu_custom_call" | custom-call | flops 4849664000 | bytes 23000000 | tf_op jit(solution)/shard_map/backward/pallas_call | solution.py:407
  44.0 2.8 %collective-permute-start = (bf16[8,80,256]{2,1,0:T(8,128)(2,1)S(1)}, bf16[8,80,256]{2,1,0:T(8,128)(2,1)S(1)}, u32[]{:S(2)}, u32[]{:S(2)}) collective-permute-start(bf16[8,80,256]{2,1,0:T(8,128)(2,1)S(1)} %get-tuple-element.28), channel_id=1, source_target_pairs={{0,1},{1,0},{2,3},{3,2},{4,5},{5,4},{6,7},{7,6},{8,9},{9,8},{10,11... | collective-permute-start | bytes 983048 | tf_op jit(solution)/shard_map/ppermute | solution.py:473
  46.7 1.3 %collective-permute-done = bf16[8,80,256]{2,1,0:T(8,128)(2,1)S(1)} collective-permute-done((bf16[8,80,256]{2,1,0:T(8,128)(2,1)S(1)}, bf16[8,80,256]{2,1,0:T(8,128)(2,1)S(1)}, u32[]{:S(2)}, u32[]{:S(2)}) %collective-permute-start) | collective-permute-done | bytes 327712 | tf_op jit(solution)/shard_map/ppermute | solution.py:473
  48.0 0.1 add_convert_fusion
  48.1 20.9 %all_to_all.15.got_ref = bf16[8,80,256]{2,1,0:T(8,128)(2,1)} all-to-all(bf16[8,80,256]{2,1,0:T(8,128)(2,1)S(1)} %add_convert_fusion), channel_id=1, replica_groups={{0,2,4,6,8,10,12,14},{1,3,5,7,9,11,13,15},{16,18,20,22,24,26,28,30},{17..., dimensions={0} | all-to-all | bytes 655360 | tf_op jit(solution)/shard_map/all_to_all | solution.py:476
  69.0 1.7 %total.1 = (f32[1,8,256]{2,1,0:T(8,128)}, f32[1,4,16,256]{3,2,1,0:T(8,128)}, f32[1,4,16]{2,1,0:T(4,128)}) custom-call(bf16[8,80,256]{2,1,0:T(8,128)(2,1)} %all_to_all.15.got_ref), custom_call_target="tpu_custom_call" | custom-call | tf_op jit(solution)/shard_map/total/pallas_call | solution.py:441
  (2 shorter events, 0.0 us)
Async XLA Ops:
  2.6 14.1 %all-to-all-start = ((f32[16,8,128]{2,1,0:T(8,128)}), f32[16,8,128]{2,1,0:T(8,128)S(1)}, u32[]{:S(2)}, u32[]{:S(2)}) async-start(f32[16,8,128]{2,1,0:T(8,128)} %bitcast.20), calls=%async_computation | async-start | bytes 131072 | tf_op jit(solution)/shard_map/all_to_all | solution.py:466
  24.3 10.7 %all-to-all-start.1 = ((f32[16,8,128]{2,1,0:T(8,128)}), f32[16,8,128]{2,1,0:T(8,128)S(1)}, u32[]{:S(2)}, u32[]{:S(2)}) async-start(f32[16,8,128]{2,1,0:T(8,128)} %get-tuple-element.20), calls=%async_computation.1 | async-start | bytes 131072 | tf_op jit(solution)/shard_map/all_to_all | solution.py:470
  44.0 4.0 %collective-permute-start = (bf16[8,80,256]{2,1,0:T(8,128)(2,1)S(1)}, bf16[8,80,256]{2,1,0:T(8,128)(2,1)S(1)}, u32[]{:S(2)}, u32[]{:S(2)}) collective-permute-start(bf16[8,80,256]{2,1,0:T(8,128)(2,1)S(1)} %get-tuple-element.28), channel_id=1, source_target_pairs={{0,1},{1,0},{2,3},{3,2},{4,5},{5,4},{6,7},{7,6},{8,9},{9,8},{10,11... | collective-permute-start | bytes 983048 | tf_op jit(solution)/shard_map/ppermute | solution.py:473

commit v2 on v1

--- a/solution.py
+++ b/solution.py
@@ -145,7 +145,7 @@
 def forward_kernel(
     recv_ref, meta_ref, freq_ref, win_ref, wh_ref, head_ref,
     send_ref, enc_ref, half_ref, local_ref,
-    pos_ref, raw_ref, meta_copy, halves, encoded, local, sem, out_sem, *, chunk,
+    pos_ref, raw_ref, meta_copy, halves, encoded, local, send, sem, out_sem, *, chunk,
 ):
     meta = pltpu.make_async_copy(meta_ref, meta_copy, sem)
     meta.start()
@@ -168,8 +168,14 @@
             half = dot(weight, acts[i])
             acts[i] = (half + half * jnp.tanh(half)).astype(BF16)
             halves[index, :, start : start + chunk] = half.astype(BF16)
-        copies.append(pltpu.make_async_copy(halves.at[index], half_ref.at[index], out_sem.at[index]))
-        copies[-1].start()
+            if index == LAYERS:
+                cut = pl.ds(start, chunk)
+                at = out_sem.at[LAYERS + 3 + i] if i else out_sem.at[LAYERS]
+                copies.append(pltpu.make_async_copy(halves.at[index, :, cut], half_ref.at[index, :, cut], at))
+                copies[-1].start()
+        if index < LAYERS:
+            copies.append(pltpu.make_async_copy(halves.at[index], half_ref.at[index], out_sem.at[index]))
+            copies[-1].start()
     for i, act in enumerate(acts):
         raw = dot(head_ref[...], act)
         for t in range(count):
@@ -183,7 +189,9 @@
     meta.wait()
     block = jnp.concatenate(rows + [meta_copy[4:8, :]], axis=0)
     for r in range(REGIONS):
-        send_ref[r] = block
+        send[r] = block
+    copies.append(pltpu.make_async_copy(send, send_ref, out_sem.at[LAYERS + 3]))
+    copies[-1].start()
     steep = (0.5 + 0.5 * jnp.tanh(0.5 * raw[0])) * spacing
     local[0] = transmit * fade * steep
     local[1] = steep
@@ -214,12 +222,12 @@
         kernel,
         in_specs=specs,
         out_shape=(
-            jax.ShapeDtypeStruct((REGIONS, 8, SLOTS), F32),
+            pltpu.HBM((REGIONS, 8, SLOTS), F32),
             pltpu.HBM((ENC, ROWS), BF16),
             pltpu.HBM((LAYERS + 1, HID, ROWS), BF16),
             pltpu.HBM((9, SEG_LEN, SLOTS), F32),
         ),
-        out_specs=tuple(in_vmem(1) + in_hbm(3)),
+        out_specs=tuple(in_hbm(4)),
         scratch_shapes=[
             pltpu.VMEM((128, SLOTS), F32),
             pltpu.VMEM((4, SEG_LEN, SLOTS), F32),
@@ -227,8 +235,9 @@
             pltpu.VMEM((LAYERS + 1, HID, ROWS), BF16),
             pltpu.VMEM((ENC, ROWS), BF16),
             pltpu.VMEM((9, SEG_LEN, SLOTS), F32),
+            pltpu.VMEM((REGIONS, 8, SLOTS), F32),
             pltpu.SemaphoreType.DMA,
-            pltpu.SemaphoreType.DMA((LAYERS + 3,)),
+            pltpu.SemaphoreType.DMA((LAYERS + 3 + ROWS // chunk,)),
         ],
         compiler_params=pltpu.CompilerParams(vmem_limit_bytes=VMEM_LIMIT),
         cost_estimate=pl.CostEstimate(flops=2 * ROWS * 296000, bytes_accessed=700000, transcendentals=ROWS * 1280),

time: 71.2 us -> 70.3 us (0.987)
  Pallas kernels: 21.8 us -> 20.9 us
    pallas_call x1, Pallas kernels: 7.57 us -> 6.65 us  [forward_call(): pl.pallas_call(kernel, in_specs=specs, out_shape=(pltpu.HBM((REGIONS, 8,...]
where the time goes in v2:
time: 70.3 us; the launch traced here: 69.7 us
  Pallas kernels  20.9 us (30%)
  blocking collectives  20.9 us (30%)
  starting transfers between devices  14.5 us (21%)
  waiting for transfers between devices  8.63 us (12%)
  local copies, waits for them, and re-layouts  2.83 us (4%)
  other arithmetic  1.25 us (2%)
  between operations  0.71 us (1%)
    all_to_all x1, blocking collectives, per_device(): lax.all_to_all(both, 'dp', 0, 0, tiled=True, axis_index_groups=groups)  20.9 us
    pallas_call x1, Pallas kernels, backward_call(): pl.pallas_call(kernel, in_specs=in_vmem(5) + in_hbm(2), out_shape=(jax.Sh...  8.93 us
    all_to_all x1, starting transfers between devices, per_device(): lax.all_to_all(outgoing.reshape(REGIONS, CAP, 128), 'region', split_axis=...  7.58 us
    pallas_call x1, Pallas kernels, forward_call(): pl.pallas_call(kernel, in_specs=specs, out_shape=(pltpu.HBM((REGIONS, 8,...  6.65 us
    all_to_all x1, waiting for transfers between devices, per_device(): lax.all_to_all(summary, 'region', split_axis=0, concat_axis=0, tiled=True)  4.89 us
    all_to_all x1, starting transfers between devices, per_device(): lax.all_to_all(summary, 'region', split_axis=0, concat_axis=0, tiled=True)  4.2 us
    ppermute x1, starting transfers between devices, per_device(): other = lax.ppermute(send, 'dp', [(i, i ^ 1) for i in range(16)])  2.76 us
    unnamed x3, local copies, waits for them, and re-layouts  2.54 us
  transfers between devices with their start and end apart: 3, of which 3 were waited for; matrix products, arithmetic and copies ran while one was open for 6% of the time, Pallas kernels for 2%

profile of v2, /device:TPU:1, one launch (start us, length us, event | category | flops | bytes accessed | tf_op | source)
XLA Modules:
  0.0 69.7 jit_solution(7321980224544574494)
XLA Ops:
  0.6 2.0 %dispatch.1 = (f32[128,128]{1,0:T(8,128)}, f32[8,128]{1,0:T(8,128)}) custom-call(f32[3,16,128]{2,1,0:T(8,128)} %pos_ref.1, f32[16,128]{1,0:T(8,128)} %sp_ref.1, f32[3,16]{1,0:T(4,128)} %tg_ref.1, s32[1,64]{1,0:T(1,128)} %bitcast.21), custom_call_target="tpu_custom_call" | custom-call | tf_op jit(solution)/shard_map/dispatch/pallas_call | solution.py:95
  2.6 7.6 %all-to-all-start = ((f32[16,8,128]{2,1,0:T(8,128)}), f32[16,8,128]{2,1,0:T(8,128)S(1)}, u32[]{:S(2)}, u32[]{:S(2)}) async-start(f32[16,8,128]{2,1,0:T(8,128)} %bitcast.20), calls=%async_computation | async-start | bytes 131072 | tf_op jit(solution)/shard_map/all_to_all | solution.py:475
  10.2 0.8 %copy.12 = f32[3,64]{0,1:T(8,128)S(1)} copy(f32[3,64]{1,0:T(4,128)} %param.11) | data formatting | bytes 1536 | tf_op args[3]
  11.0 0.9 %copy.13 = bf16[1,128,256]{1,2,0:T(8,128)(2,1)S(1)} copy(bf16[1,128,256]{2,1,0:T(8,128)(2,1)} %param.13) | data formatting | bytes 131072 | tf_op args[5]
  12.0 0.8 %copy.14 = bf16[1,4,256]{1,2,0:T(8,128)(2,1)S(1)} copy(bf16[1,4,256]{2,1,0:T(4,128)(2,1)} %param.15) | data formatting | bytes 4096 | tf_op args[7]
  12.8 0.1 copy.16.refs_5_
  12.9 1.1 %multiply_bitcast_fusion.1 = (bf16[4,256,256]{2,1,0:T(8,128)(2,1)S(1)}, bf16[4,256,256]{1,2,0:T(8,128)(2,1)S(1)}) fusion(bf16[1,4,256,256]{3,2,1,0:T(8,128)(2,1)} %param.14), kind=kLoop, calls=%fused_computation.2 | loop fusion | flops 262144 | bytes 1572864 | tf_op jit(solution)/shard_map/mul | solution.py:468
  14.0 0.2 copy.15.refs_4_
  14.3 2.5 %all-to-all-done = f32[16,8,128]{2,1,0:T(8,128)S(1)} async-done(((f32[16,8,128]{2,1,0:T(8,128)}), f32[16,8,128]{2,1,0:T(8,128)S(1)}, u32[]{:S(2)}, u32[]{:S(2)}) %all-to-all-start) | async-done | bytes 65568 | tf_op jit(solution)/shard_map/all_to_all | solution.py:475
  16.8 6.7 %forward.1 = (f32[16,8,128]{2,1,0:T(8,128)}, bf16[128,4096]{1,0:T(8,128)(2,1)}, bf16[5,256,4096]{2,1,0:T(8,128)(2,1)}, f32[9,32,128]{2,1,0:T(8,128)}) custom-call(f32[128,128]{1,0:T(8,128)S(1)} %bitcast.16, f32[8,128]{1,0:T(8,128)} %get-tuple-element.19.refs_1_, f32[64,3]{1,0:T(8,128)S(1)} %bitcast.17, bf16[256,128]{1,0:T(8,128)(2,1)S(1)} %multiply_bitcast_fusion.3.refs_3_, ...), custom_call_target="tpu_custom_call" | custom-call | flops 2424832000 | bytes 700000 | tf_op jit(solution)/shard_map/forward/pallas_call | solution.py:221
  23.4 4.2 %all-to-all-start.1 = ((f32[16,8,128]{2,1,0:T(8,128)}), f32[16,8,128]{2,1,0:T(8,128)S(1)}, u32[]{:S(2)}, u32[]{:S(2)}) async-start(f32[16,8,128]{2,1,0:T(8,128)} %get-tuple-element.20), calls=%async_computation.1 | async-start | bytes 131072 | tf_op jit(solution)/shard_map/all_to_all | solution.py:479
  27.6 1.6 %fetch.1 = (f32[9,32,128]{2,1,0:T(8,128)S(1)}, bf16[256,4096]{1,0:T(8,128)(2,1)S(1)}) custom-call(f32[9,32,128]{2,1,0:T(8,128)} %get-tuple-element.21.local_in, bf16[5,256,4096]{2,1,0:T(8,128)(2,1)} %get-tuple-element.22.half_in.refs_6_), custom_call_target="tpu_custom_call" | custom-call | flops 2000000000 | bytes 20000000 | tf_op jit(solution)/shard_map/fetch/pallas_call | solution.py:332
  29.2 4.9 %all-to-all-done.1.refs_0_ = f32[16,8,128]{2,1,0:T(8,128)S(1)} async-done(((f32[16,8,128]{2,1,0:T(8,128)}), f32[16,8,128]{2,1,0:T(8,128)S(1)}, u32[]{:S(2)}, u32[]{:S(2)}) %all-to-all-start.1) | async-done | bytes 65568 | tf_op jit(solution)/shard_map/all_to_all | solution.py:479
  34.1 8.9 %backward.1 = (f32[3,16]{1,0:T(4,128)}, bf16[8,80,256]{2,1,0:T(8,128)(2,1)S(1)}, bf16[8,80,256]{2,1,0:T(8,128)(2,1)S(1)}) custom-call(f32[16,8,128]{2,1,0:T(8,128)S(1)} %all-to-all-done.1.refs_0_, bf16[4,256,256]{2,1,0:T(8,128)(2,1)S(1)} %get-tuple-element.32.refs_1_, bf16[256,8]{1,0:T(8,128)(2,1)S(1)} %multiply_bitcast_fusion.2.refs_2_, ...), custom_call_target="tpu_custom_call" | custom-call | flops 4849664000 | bytes 23000000 | tf_op jit(solution)/shard_map/backward/pallas_call | solution.py:416
  43.1 2.8 %collective-permute-start = (bf16[8,80,256]{2,1,0:T(8,128)(2,1)S(1)}, bf16[8,80,256]{2,1,0:T(8,128)(2,1)S(1)}, u32[]{:S(2)}, u32[]{:S(2)}) collective-permute-start(bf16[8,80,256]{2,1,0:T(8,128)(2,1)S(1)} %get-tuple-element.28), channel_id=1, source_target_pairs={{0,1},{1,0},{2,3},{3,2},{4,5},{5,4},{6,7},{7,6},{8,9},{9,8},{10,11... | collective-permute-start | bytes 983048 | tf_op jit(solution)/shard_map/ppermute | solution.py:482
  45.8 1.3 %collective-permute-done = bf16[8,80,256]{2,1,0:T(8,128)(2,1)S(1)} collective-permute-done((bf16[8,80,256]{2,1,0:T(8,128)(2,1)S(1)}, bf16[8,80,256]{2,1,0:T(8,128)(2,1)S(1)}, u32[]{:S(2)}, u32[]{:S(2)}) %collective-permute-start) | collective-permute-done | bytes 327712 | tf_op jit(solution)/shard_map/ppermute | solution.py:482
  47.1 0.1 add_convert_fusion
  47.2 20.9 %all_to_all.15.got_ref = bf16[8,80,256]{2,1,0:T(8,128)(2,1)} all-to-all(bf16[8,80,256]{2,1,0:T(8,128)(2,1)S(1)} %add_convert_fusion), channel_id=1, replica_groups={{0,2,4,6,8,10,12,14},{1,3,5,7,9,11,13,15},{16,18,20,22,24,26,28,30},{17..., dimensions={0} | all-to-all | bytes 655360 | tf_op jit(solution)/shard_map/all_to_all | solution.py:485
  68.0 1.7 %total.1 = (f32[1,8,256]{2,1,0:T(8,128)}, f32[1,4,16,256]{3,2,1,0:T(8,128)}, f32[1,4,16]{2,1,0:T(4,128)}) custom-call(bf16[8,80,256]{2,1,0:T(8,128)(2,1)} %all_to_all.15.got_ref), custom_call_target="tpu_custom_call" | custom-call | tf_op jit(solution)/shard_map/total/pallas_call | solution.py:450
  (2 shorter events, 0.0 us)
Async XLA Ops:
  2.6 14.1 %all-to-all-start = ((f32[16,8,128]{2,1,0:T(8,128)}), f32[16,8,128]{2,1,0:T(8,128)S(1)}, u32[]{:S(2)}, u32[]{:S(2)}) async-start(f32[16,8,128]{2,1,0:T(8,128)} %bitcast.20), calls=%async_computation | async-start | bytes 131072 | tf_op jit(solution)/shard_map/all_to_all | solution.py:475
  23.4 10.7 %all-to-all-start.1 = ((f32[16,8,128]{2,1,0:T(8,128)}), f32[16,8,128]{2,1,0:T(8,128)S(1)}, u32[]{:S(2)}, u32[]{:S(2)}) async-start(f32[16,8,128]{2,1,0:T(8,128)} %get-tuple-element.20), calls=%async_computation.1 | async-start | bytes 131072 | tf_op jit(solution)/shard_map/all_to_all | solution.py:479
  43.1 4.0 %collective-permute-start = (bf16[8,80,256]{2,1,0:T(8,128)(2,1)S(1)}, bf16[8,80,256]{2,1,0:T(8,128)(2,1)S(1)}, u32[]{:S(2)}, u32[]{:S(2)}) collective-permute-start(bf16[8,80,256]{2,1,0:T(8,128)(2,1)S(1)} %get-tuple-element.28), channel_id=1, source_target_pairs={{0,1},{1,0},{2,3},{3,2},{4,5},{5,4},{6,7},{7,6},{8,9},{9,8},{10,11... | collective-permute-start | bytes 983048 | tf_op jit(solution)/shard_map/ppermute | solution.py:482

commit v3 on v2

--- a/solution.py
+++ b/solution.py
@@ -12,7 +12,6 @@
 BF16 = jnp.bfloat16
 NN = (((1,), (0,)), ((), ()))
 NT = (((1,), (1,)), ((), ()))
-TN = (((0,), (0,)), ((), ()))
 VMEM_LIMIT = 40 * 1024 * 1024
 BACK_LIMIT = 24 * 1024 * 1024
 
@@ -64,15 +63,14 @@
 
 def dispatch_kernel(pos_ref, sp_ref, tg_ref, seg_ref, send_ref, meta_ref):
     parity = lax.axis_index("region") % 2
-    lane = iota((SEGS, SLOTS), 1)
-    row = iota((SEGS, SEGS), 0)
-    order = as_mask(iota((SEGS, SEGS), 1) == (row % RAYS_DEV) * 4 + row // RAYS_DEV)
-    seg = dot(order, jnp.broadcast_to(seg_ref[...], (8, SEGS)).astype(F32).astype(BF16), NT)[:, 0:1]
-    member = jnp.where(seg == lane.astype(F32), 1.0, 0.0)
-    earlier = as_mask(iota((SEGS, SEGS), 1) < row)
-    rank = dot(earlier, member.astype(BF16))
-    slot = jnp.sum(member * (rank + (lane * CAP).astype(F32)), axis=1, keepdims=True)
-    onehot = as_mask(slot == lane.astype(F32))
+    at = iota((SEGS, SEGS), 1)
+    order = as_mask(iota((SEGS, SEGS), 0) == (at % RAYS_DEV) * 4 + at // RAYS_DEV)
+    seg = dot(jnp.broadcast_to(seg_ref[...], (REGIONS, SEGS)).astype(F32).astype(BF16), order)
+    region = iota((REGIONS, SEGS), 0).astype(F32)
+    member = seg == region
+    rank = dot(as_mask(member), as_mask(iota((SEGS, SEGS), 0) < at))
+    slot = jnp.sum(jnp.where(member, rank + region * CAP, 0.0), axis=0, keepdims=True)
+    onehot = as_mask(iota((SLOTS, SEGS), 0).astype(F32) == slot)
     parts = []
     for q in range(4):
         cut = slice(q * SEG_LEN, (q + 1) * SEG_LEN)
@@ -82,13 +80,12 @@
             )
         )
     data = jnp.concatenate(parts, axis=0)
-    send_ref[...] = pick_left(onehot, data, TN)
-    ids = dot(iota((8, SLOTS), 1).astype(BF16), onehot, NT)
+    send_ref[...] = pick_left(onehot, data, NN)
     half = iota((8, 128), 1) // SEGS == parity
-    ids = jnp.concatenate([ids, ids], axis=1)
+    ids = jnp.broadcast_to(jnp.concatenate([slot, slot], axis=1), (5, 128))
     spread = as_mask(iota((RAYS_DEV, 128), 1) % RAYS_DEV == iota((RAYS_DEV, 128), 0))
     tg = pick(jnp.concatenate([tg_ref[...], tg_ref[...], tg_ref[0:2, :]], axis=0), spread, NN)
-    meta_ref[...] = jnp.where(half, jnp.concatenate([ids[0:4], ids[0:1], tg[0:3]], axis=0), 0.0)
+    meta_ref[...] = jnp.where(half, jnp.concatenate([ids, tg[0:3]], axis=0), 0.0)
 
 
 def dispatch(positions, spacing, targets, seg_region):

time: 70.3 us -> 70.1 us (level)
  no operation moved by 1% of the time
where the time goes in v3:
time: 70.1 us; the launch traced here: 69.5 us
  blocking collectives  20.9 us (30%)
  Pallas kernels  20.7 us (30%)
  starting transfers between devices  14.5 us (21%)
  waiting for transfers between devices  8.63 us (12%)
  local copies, waits for them, and re-layouts  2.83 us (4%)
  other arithmetic  1.25 us (2%)
  between operations  0.71 us (1%)
    all_to_all x1, blocking collectives, per_device(): lax.all_to_all(both, 'dp', 0, 0, tiled=True, axis_index_groups=groups)  20.9 us
    pallas_call x1, Pallas kernels, backward_call(): pl.pallas_call(kernel, in_specs=in_vmem(5) + in_hbm(2), out_shape=(jax.Sh...  8.92 us
    all_to_all x1, starting transfers between devices, per_device(): lax.all_to_all(outgoing.reshape(REGIONS, CAP, 128), 'region', split_axis=...  7.58 us
    pallas_call x1, Pallas kernels, forward_call(): pl.pallas_call(kernel, in_specs=specs, out_shape=(pltpu.HBM((REGIONS, 8,...  6.65 us
    all_to_all x1, waiting for transfers between devices, per_device(): lax.all_to_all(summary, 'region', split_axis=0, concat_axis=0, tiled=True)  4.89 us
    all_to_all x1, starting transfers between devices, per_device(): lax.all_to_all(summary, 'region', split_axis=0, concat_axis=0, tiled=True)  4.2 us
    ppermute x1, starting transfers between devices, per_device(): other = lax.ppermute(send, 'dp', [(i, i ^ 1) for i in range(16)])  2.75 us
    unnamed x3, local copies, waits for them, and re-layouts  2.54 us
  transfers between devices with their start and end apart: 3, of which 3 were waited for; matrix products, arithmetic and copies ran while one was open for 6% of the time, Pallas kernels for 2%

profile of v3, /device:TPU:1, one launch (start us, length us, event | category | flops | bytes accessed | tf_op | source)
XLA Modules:
  0.0 69.5 jit_solution(8274779532788149152)
XLA Ops:
  0.6 1.8 %dispatch.1 = (f32[128,128]{1,0:T(8,128)}, f32[8,128]{1,0:T(8,128)}) custom-call(f32[3,16,128]{2,1,0:T(8,128)} %pos_ref.1, f32[16,128]{1,0:T(8,128)} %sp_ref.1, f32[3,16]{1,0:T(4,128)} %tg_ref.1, s32[1,64]{1,0:T(1,128)} %bitcast.21), custom_call_target="tpu_custom_call" | custom-call | tf_op jit(solution)/shard_map/dispatch/pallas_call | solution.py:92
  2.4 7.6 %all-to-all-start = ((f32[16,8,128]{2,1,0:T(8,128)}), f32[16,8,128]{2,1,0:T(8,128)S(1)}, u32[]{:S(2)}, u32[]{:S(2)}) async-start(f32[16,8,128]{2,1,0:T(8,128)} %bitcast.20), calls=%async_computation | async-start | bytes 131072 | tf_op jit(solution)/shard_map/all_to_all | solution.py:472
  10.0 0.8 %copy.12 = f32[3,64]{0,1:T(8,128)S(1)} copy(f32[3,64]{1,0:T(4,128)} %param.11) | data formatting | bytes 1536 | tf_op args[3]
  10.8 0.9 %copy.13 = bf16[1,128,256]{1,2,0:T(8,128)(2,1)S(1)} copy(bf16[1,128,256]{2,1,0:T(8,128)(2,1)} %param.13) | data formatting | bytes 131072 | tf_op args[5]
  11.8 0.8 %copy.14 = bf16[1,4,256]{1,2,0:T(8,128)(2,1)S(1)} copy(bf16[1,4,256]{2,1,0:T(4,128)(2,1)} %param.15) | data formatting | bytes 4096 | tf_op args[7]
  12.6 0.1 copy.16.refs_5_
  12.7 1.1 %multiply_bitcast_fusion.1 = (bf16[4,256,256]{2,1,0:T(8,128)(2,1)S(1)}, bf16[4,256,256]{1,2,0:T(8,128)(2,1)S(1)}) fusion(bf16[1,4,256,256]{3,2,1,0:T(8,128)(2,1)} %param.14), kind=kLoop, calls=%fused_computation.2 | loop fusion | flops 262144 | bytes 1572864 | tf_op jit(solution)/shard_map/mul | solution.py:465
  13.8 0.2 copy.15.refs_4_
  14.1 2.5 %all-to-all-done = f32[16,8,128]{2,1,0:T(8,128)S(1)} async-done(((f32[16,8,128]{2,1,0:T(8,128)}), f32[16,8,128]{2,1,0:T(8,128)S(1)}, u32[]{:S(2)}, u32[]{:S(2)}) %all-to-all-start) | async-done | bytes 65568 | tf_op jit(solution)/shard_map/all_to_all | solution.py:472
  16.5 6.7 %forward.1 = (f32[16,8,128]{2,1,0:T(8,128)}, bf16[128,4096]{1,0:T(8,128)(2,1)}, bf16[5,256,4096]{2,1,0:T(8,128)(2,1)}, f32[9,32,128]{2,1,0:T(8,128)}) custom-call(f32[128,128]{1,0:T(8,128)S(1)} %bitcast.16, f32[8,128]{1,0:T(8,128)} %get-tuple-element.19.refs_1_, f32[64,3]{1,0:T(8,128)S(1)} %bitcast.17, bf16[256,128]{1,0:T(8,128)(2,1)S(1)} %multiply_bitcast_fusion.3.refs_3_, ...), custom_call_target="tpu_custom_call" | custom-call | flops 2424832000 | bytes 700000 | tf_op jit(solution)/shard_map/forward/pallas_call | solution.py:218
  23.2 4.2 %all-to-all-start.1 = ((f32[16,8,128]{2,1,0:T(8,128)}), f32[16,8,128]{2,1,0:T(8,128)S(1)}, u32[]{:S(2)}, u32[]{:S(2)}) async-start(f32[16,8,128]{2,1,0:T(8,128)} %get-tuple-element.20), calls=%async_computation.1 | async-start | bytes 131072 | tf_op jit(solution)/shard_map/all_to_all | solution.py:476
  27.4 1.6 %fetch.1 = (f32[9,32,128]{2,1,0:T(8,128)S(1)}, bf16[256,4096]{1,0:T(8,128)(2,1)S(1)}) custom-call(f32[9,32,128]{2,1,0:T(8,128)} %get-tuple-element.21.local_in, bf16[5,256,4096]{2,1,0:T(8,128)(2,1)} %get-tuple-element.22.half_in.refs_6_), custom_call_target="tpu_custom_call" | custom-call | flops 2000000000 | bytes 20000000 | tf_op jit(solution)/shard_map/fetch/pallas_call | solution.py:329
  29.0 4.9 %all-to-all-done.1.refs_0_ = f32[16,8,128]{2,1,0:T(8,128)S(1)} async-done(((f32[16,8,128]{2,1,0:T(8,128)}), f32[16,8,128]{2,1,0:T(8,128)S(1)}, u32[]{:S(2)}, u32[]{:S(2)}) %all-to-all-start.1) | async-done | bytes 65568 | tf_op jit(solution)/shard_map/all_to_all | solution.py:476
  33.9 8.9 %backward.1 = (f32[3,16]{1,0:T(4,128)}, bf16[8,80,256]{2,1,0:T(8,128)(2,1)S(1)}, bf16[8,80,256]{2,1,0:T(8,128)(2,1)S(1)}) custom-call(f32[16,8,128]{2,1,0:T(8,128)S(1)} %all-to-all-done.1.refs_0_, bf16[4,256,256]{2,1,0:T(8,128)(2,1)S(1)} %get-tuple-element.32.refs_1_, bf16[256,8]{1,0:T(8,128)(2,1)S(1)} %multiply_bitcast_fusion.2.refs_2_, ...), custom_call_target="tpu_custom_call" | custom-call | flops 4849664000 | bytes 23000000 | tf_op jit(solution)/shard_map/backward/pallas_call | solution.py:413
  42.9 2.8 %collective-permute-start = (bf16[8,80,256]{2,1,0:T(8,128)(2,1)S(1)}, bf16[8,80,256]{2,1,0:T(8,128)(2,1)S(1)}, u32[]{:S(2)}, u32[]{:S(2)}) collective-permute-start(bf16[8,80,256]{2,1,0:T(8,128)(2,1)S(1)} %get-tuple-element.28), channel_id=1, source_target_pairs={{0,1},{1,0},{2,3},{3,2},{4,5},{5,4},{6,7},{7,6},{8,9},{9,8},{10,11... | collective-permute-start | bytes 983048 | tf_op jit(solution)/shard_map/ppermute | solution.py:479
  45.6 1.3 %collective-permute-done = bf16[8,80,256]{2,1,0:T(8,128)(2,1)S(1)} collective-permute-done((bf16[8,80,256]{2,1,0:T(8,128)(2,1)S(1)}, bf16[8,80,256]{2,1,0:T(8,128)(2,1)S(1)}, u32[]{:S(2)}, u32[]{:S(2)}) %collective-permute-start) | collective-permute-done | bytes 327712 | tf_op jit(solution)/shard_map/ppermute | solution.py:479
  46.9 0.1 add_convert_fusion
  47.0 20.9 %all_to_all.15.got_ref = bf16[8,80,256]{2,1,0:T(8,128)(2,1)} all-to-all(bf16[8,80,256]{2,1,0:T(8,128)(2,1)S(1)} %add_convert_fusion), channel_id=1, replica_groups={{0,2,4,6,8,10,12,14},{1,3,5,7,9,11,13,15},{16,18,20,22,24,26,28,30},{17..., dimensions={0} | all-to-all | bytes 655360 | tf_op jit(solution)/shard_map/all_to_all | solution.py:482
  67.8 1.7 %total.1 = (f32[1,8,256]{2,1,0:T(8,128)}, f32[1,4,16,256]{3,2,1,0:T(8,128)}, f32[1,4,16]{2,1,0:T(4,128)}) custom-call(bf16[8,80,256]{2,1,0:T(8,128)(2,1)} %all_to_all.15.got_ref), custom_call_target="tpu_custom_call" | custom-call | tf_op jit(solution)/shard_map/total/pallas_call | solution.py:447
  (2 shorter events, 0.0 us)
Async XLA Ops:
  2.4 14.1 %all-to-all-start = ((f32[16,8,128]{2,1,0:T(8,128)}), f32[16,8,128]{2,1,0:T(8,128)S(1)}, u32[]{:S(2)}, u32[]{:S(2)}) async-start(f32[16,8,128]{2,1,0:T(8,128)} %bitcast.20), calls=%async_computation | async-start | bytes 131072 | tf_op jit(solution)/shard_map/all_to_all | solution.py:472
  23.2 10.7 %all-to-all-start.1 = ((f32[16,8,128]{2,1,0:T(8,128)}), f32[16,8,128]{2,1,0:T(8,128)S(1)}, u32[]{:S(2)}, u32[]{:S(2)}) async-start(f32[16,8,128]{2,1,0:T(8,128)} %get-tuple-element.20), calls=%async_computation.1 | async-start | bytes 131072 | tf_op jit(solution)/shard_map/all_to_all | solution.py:476
  42.9 4.0 %collective-permute-start = (bf16[8,80,256]{2,1,0:T(8,128)(2,1)S(1)}, bf16[8,80,256]{2,1,0:T(8,128)(2,1)S(1)}, u32[]{:S(2)}, u32[]{:S(2)}) collective-permute-start(bf16[8,80,256]{2,1,0:T(8,128)(2,1)S(1)} %get-tuple-element.28), channel_id=1, source_target_pairs={{0,1},{1,0},{2,3},{3,2},{4,5},{5,4},{6,7},{7,6},{8,9},{9,8},{10,11... | collective-permute-start | bytes 983048 | tf_op jit(solution)/shard_map/ppermute | solution.py:479

commit v4 on v3

--- a/solution.py
+++ b/solution.py
@@ -379,6 +379,7 @@
         act, slope = residual(LAYERS, cut)
         slopes.append(slope)
         ghead = ghead + dot(up, act, NT)
+    core = lax.axis_index("dp") % 2
     for index in range(LAYERS, -1, -1):
         for copy in {LAYERS: copies[LAYERS - 1 : LAYERS], LAYERS - 1: copies[1 : LAYERS - 1], 1: [copies[0], copies[LAYERS]]}.get(index, []):
             copy.wait()
@@ -396,15 +397,15 @@
             gh_ref[index - 1] = total
         else:
             gin_ref[...] = total
-    core = lax.axis_index("dp") % 2
-    for ref, which in ((keep_ref, core), (send_ref, 1 - core)):
-        for z in range(8):
-            to = z * 2 + which
-            for l in range(LAYERS):
-                rows = gh_ref[l, pl.ds(pl.multiple_of(to * 16, 16), 16), :]
-                ref[z, l * 16 : (l + 1) * 16, :] = rows.astype(BF16)
-            rows = gin_ref[pl.ds(pl.multiple_of(to * 8, 8), 8), :]
-            ref[z, 64:80, :] = jnp.concatenate([rows, ghead], axis=0).astype(BF16)
+        for ref, which in ((keep_ref, core), (send_ref, 1 - core)):
+            for z in range(8):
+                to = z * 2 + which
+                if index > 0:
+                    rows = gh_ref[index - 1, pl.ds(pl.multiple_of(to * 16, 16), 16), :]
+                    ref[z, (index - 1) * 16 : index * 16, :] = rows.astype(BF16)
+                else:
+                    rows = gin_ref[pl.ds(pl.multiple_of(to * 8, 8), 8), :]
+                    ref[z, 64:80, :] = jnp.concatenate([rows, ghead], axis=0).astype(BF16)
 
 
 def backward_call(got, wh, head, local, top, enc, half, gain, chunk=512):

time: 70.1 us -> 71.5 us (1.020)
  Pallas kernels: 20.7 us -> 22.2 us
    pallas_call x1, Pallas kernels: 8.92 us -> 10.4 us  [backward_call(): pl.pallas_call(kernel, in_specs=in_vmem(5) + in_hbm(2), out_shape=(jax.Sh...]
where the time goes in v4:
time: 71.5 us; the launch traced here: 71 us
  Pallas kernels  22.2 us (31%)
  blocking collectives  20.9 us (29%)
  starting transfers between devices  14.5 us (20%)
  waiting for transfers between devices  8.63 us (12%)
  local copies, waits for them, and re-layouts  2.83 us (4%)
  other arithmetic  1.25 us (2%)
    all_to_all x1, blocking collectives, per_device(): lax.all_to_all(both, 'dp', 0, 0, tiled=True, axis_index_groups=groups)  20.9 us
    pallas_call x1, Pallas kernels, backward_call(): pl.pallas_call(kernel, in_specs=in_vmem(5) + in_hbm(2), out_shape=(jax.Sh...  10.4 us
    all_to_all x1, starting transfers between devices, per_device(): lax.all_to_all(outgoing.reshape(REGIONS, CAP, 128), 'region', split_axis=...  7.58 us
    pallas_call x1, Pallas kernels, forward_call(): pl.pallas_call(kernel, in_specs=specs, out_shape=(pltpu.HBM((REGIONS, 8,...  6.65 us
    all_to_all x1, waiting for transfers between devices, per_device(): lax.all_to_all(summary, 'region', split_axis=0, concat_axis=0, tiled=True)  4.89 us
    all_to_all x1, starting transfers between devices, per_device(): lax.all_to_all(summary, 'region', split_axis=0, concat_axis=0, tiled=True)  4.2 us
    ppermute x1, starting transfers between devices, per_device(): other = lax.ppermute(send, 'dp', [(i, i ^ 1) for i in range(16)])  2.75 us
    unnamed x3, local copies, waits for them, and re-layouts  2.54 us
  transfers between devices with their start and end apart: 3, of which 3 were waited for; matrix products, arithmetic and copies ran while one was open for 6% of the time, Pallas kernels for 2%

profile of v4, /device:TPU:1, one launch (start us, length us, event | category | flops | bytes accessed | tf_op | source)
XLA Modules:
  0.0 71.0 jit_solution(17930848541238743237)
XLA Ops:
  0.6 1.8 %dispatch.1 = (f32[128,128]{1,0:T(8,128)}, f32[8,128]{1,0:T(8,128)}) custom-call(f32[3,16,128]{2,1,0:T(8,128)} %pos_ref.1, f32[16,128]{1,0:T(8,128)} %sp_ref.1, f32[3,16]{1,0:T(4,128)} %tg_ref.1, s32[1,64]{1,0:T(1,128)} %bitcast.21), custom_call_target="tpu_custom_call" | custom-call | tf_op jit(solution)/shard_map/dispatch/pallas_call | solution.py:92
  2.4 7.6 %all-to-all-start = ((f32[16,8,128]{2,1,0:T(8,128)}), f32[16,8,128]{2,1,0:T(8,128)S(1)}, u32[]{:S(2)}, u32[]{:S(2)}) async-start(f32[16,8,128]{2,1,0:T(8,128)} %bitcast.20), calls=%async_computation | async-start | bytes 131072 | tf_op jit(solution)/shard_map/all_to_all | solution.py:473
  10.0 0.8 %copy.12 = f32[3,64]{0,1:T(8,128)S(1)} copy(f32[3,64]{1,0:T(4,128)} %param.11) | data formatting | bytes 1536 | tf_op args[3]
  10.8 0.9 %copy.13 = bf16[1,128,256]{1,2,0:T(8,128)(2,1)S(1)} copy(bf16[1,128,256]{2,1,0:T(8,128)(2,1)} %param.13) | data formatting | bytes 131072 | tf_op args[5]
  11.8 0.8 %copy.14 = bf16[1,4,256]{1,2,0:T(8,128)(2,1)S(1)} copy(bf16[1,4,256]{2,1,0:T(4,128)(2,1)} %param.15) | data formatting | bytes 4096 | tf_op args[7]
  12.6 0.1 copy.16.refs_5_
  12.7 1.1 %multiply_bitcast_fusion.1 = (bf16[4,256,256]{2,1,0:T(8,128)(2,1)S(1)}, bf16[4,256,256]{1,2,0:T(8,128)(2,1)S(1)}) fusion(bf16[1,4,256,256]{3,2,1,0:T(8,128)(2,1)} %param.14), kind=kLoop, calls=%fused_computation.2 | loop fusion | flops 262144 | bytes 1572864 | tf_op jit(solution)/shard_map/mul | solution.py:466
  13.8 0.2 copy.15.refs_4_
  14.1 2.5 %all-to-all-done = f32[16,8,128]{2,1,0:T(8,128)S(1)} async-done(((f32[16,8,128]{2,1,0:T(8,128)}), f32[16,8,128]{2,1,0:T(8,128)S(1)}, u32[]{:S(2)}, u32[]{:S(2)}) %all-to-all-start) | async-done | bytes 65568 | tf_op jit(solution)/shard_map/all_to_all | solution.py:473
  16.5 6.7 %forward.1 = (f32[16,8,128]{2,1,0:T(8,128)}, bf16[128,4096]{1,0:T(8,128)(2,1)}, bf16[5,256,4096]{2,1,0:T(8,128)(2,1)}, f32[9,32,128]{2,1,0:T(8,128)}) custom-call(f32[128,128]{1,0:T(8,128)S(1)} %bitcast.16, f32[8,128]{1,0:T(8,128)} %get-tuple-element.19.refs_1_, f32[64,3]{1,0:T(8,128)S(1)} %bitcast.17, bf16[256,128]{1,0:T(8,128)(2,1)S(1)} %multiply_bitcast_fusion.3.refs_3_, ...), custom_call_target="tpu_custom_call" | custom-call | flops 2424832000 | bytes 700000 | tf_op jit(solution)/shard_map/forward/pallas_call | solution.py:218
  23.2 4.2 %all-to-all-start.1 = ((f32[16,8,128]{2,1,0:T(8,128)}), f32[16,8,128]{2,1,0:T(8,128)S(1)}, u32[]{:S(2)}, u32[]{:S(2)}) async-start(f32[16,8,128]{2,1,0:T(8,128)} %get-tuple-element.20), calls=%async_computation.1 | async-start | bytes 131072 | tf_op jit(solution)/shard_map/all_to_all | solution.py:477
  27.4 1.6 %fetch.1 = (f32[9,32,128]{2,1,0:T(8,128)S(1)}, bf16[256,4096]{1,0:T(8,128)(2,1)S(1)}) custom-call(f32[9,32,128]{2,1,0:T(8,128)} %get-tuple-element.21.local_in, bf16[5,256,4096]{2,1,0:T(8,128)(2,1)} %get-tuple-element.22.half_in.refs_6_), custom_call_target="tpu_custom_call" | custom-call | flops 2000000000 | bytes 20000000 | tf_op jit(solution)/shard_map/fetch/pallas_call | solution.py:329
  29.0 4.9 %all-to-all-done.1.refs_0_ = f32[16,8,128]{2,1,0:T(8,128)S(1)} async-done(((f32[16,8,128]{2,1,0:T(8,128)}), f32[16,8,128]{2,1,0:T(8,128)S(1)}, u32[]{:S(2)}, u32[]{:S(2)}) %all-to-all-start.1) | async-done | bytes 65568 | tf_op jit(solution)/shard_map/all_to_all | solution.py:477
  33.9 10.4 %backward.1 = (f32[3,16]{1,0:T(4,128)}, bf16[8,80,256]{2,1,0:T(8,128)(2,1)S(1)}, bf16[8,80,256]{2,1,0:T(8,128)(2,1)S(1)}) custom-call(f32[16,8,128]{2,1,0:T(8,128)S(1)} %all-to-all-done.1.refs_0_, bf16[4,256,256]{2,1,0:T(8,128)(2,1)S(1)} %get-tuple-element.32.refs_1_, bf16[256,8]{1,0:T(8,128)(2,1)S(1)} %multiply_bitcast_fusion.2.refs_2_, ...), custom_call_target="tpu_custom_call" | custom-call | flops 4849664000 | bytes 23000000 | tf_op jit(solution)/shard_map/backward/pallas_call | solution.py:414
  44.3 2.8 %collective-permute-start = (bf16[8,80,256]{2,1,0:T(8,128)(2,1)S(1)}, bf16[8,80,256]{2,1,0:T(8,128)(2,1)S(1)}, u32[]{:S(2)}, u32[]{:S(2)}) collective-permute-start(bf16[8,80,256]{2,1,0:T(8,128)(2,1)S(1)} %get-tuple-element.28), channel_id=1, source_target_pairs={{0,1},{1,0},{2,3},{3,2},{4,5},{5,4},{6,7},{7,6},{8,9},{9,8},{10,11... | collective-permute-start | bytes 983048 | tf_op jit(solution)/shard_map/ppermute | solution.py:480
  47.1 1.3 %collective-permute-done = bf16[8,80,256]{2,1,0:T(8,128)(2,1)S(1)} collective-permute-done((bf16[8,80,256]{2,1,0:T(8,128)(2,1)S(1)}, bf16[8,80,256]{2,1,0:T(8,128)(2,1)S(1)}, u32[]{:S(2)}, u32[]{:S(2)}) %collective-permute-start) | collective-permute-done | bytes 327712 | tf_op jit(solution)/shard_map/ppermute | solution.py:480
  48.3 0.1 add_convert_fusion
  48.4 20.9 %all_to_all.15.got_ref = bf16[8,80,256]{2,1,0:T(8,128)(2,1)} all-to-all(bf16[8,80,256]{2,1,0:T(8,128)(2,1)S(1)} %add_convert_fusion), channel_id=1, replica_groups={{0,2,4,6,8,10,12,14},{1,3,5,7,9,11,13,15},{16,18,20,22,24,26,28,30},{17..., dimensions={0} | all-to-all | bytes 655360 | tf_op jit(solution)/shard_map/all_to_all | solution.py:483
  69.3 1.7 %total.1 = (f32[1,8,256]{2,1,0:T(8,128)}, f32[1,4,16,256]{3,2,1,0:T(8,128)}, f32[1,4,16]{2,1,0:T(4,128)}) custom-call(bf16[8,80,256]{2,1,0:T(8,128)(2,1)} %all_to_all.15.got_ref), custom_call_target="tpu_custom_call" | custom-call | tf_op jit(solution)/shard_map/total/pallas_call | solution.py:448
  (2 shorter events, 0.0 us)
Async XLA Ops:
  2.4 14.1 %all-to-all-start = ((f32[16,8,128]{2,1,0:T(8,128)}), f32[16,8,128]{2,1,0:T(8,128)S(1)}, u32[]{:S(2)}, u32[]{:S(2)}) async-start(f32[16,8,128]{2,1,0:T(8,128)} %bitcast.20), calls=%async_computation | async-start | bytes 131072 | tf_op jit(solution)/shard_map/all_to_all | solution.py:473
  23.2 10.7 %all-to-all-start.1 = ((f32[16,8,128]{2,1,0:T(8,128)}), f32[16,8,128]{2,1,0:T(8,128)S(1)}, u32[]{:S(2)}, u32[]{:S(2)}) async-start(f32[16,8,128]{2,1,0:T(8,128)} %get-tuple-element.20), calls=%async_computation.1 | async-start | bytes 131072 | tf_op jit(solution)/shard_map/all_to_all | solution.py:477
  44.3 4.0 %collective-permute-start = (bf16[8,80,256]{2,1,0:T(8,128)(2,1)S(1)}, bf16[8,80,256]{2,1,0:T(8,128)(2,1)S(1)}, u32[]{:S(2)}, u32[]{:S(2)}) collective-permute-start(bf16[8,80,256]{2,1,0:T(8,128)(2,1)S(1)} %get-tuple-element.28), channel_id=1, source_target_pairs={{0,1},{1,0},{2,3},{3,2},{4,5},{5,4},{6,7},{7,6},{8,9},{9,8},{10,11... | collective-permute-start | bytes 983048 | tf_op jit(solution)/shard_map/ppermute | solution.py:480
